TPU v7x, 256 devices: a whole 4x4x8 slice. The times are simulated.
256 devices in a mesh: virt: 32 (over z, x_hi, core), aux: 8 (over x_lo, y).
Axes of the slice: x: 4 (x_hi: 2, x_lo: 2; x = x_hi * 2 + x_lo), y: 4, z: 8, core: 2. Of those that a mesh axis runs over, the one named last changes fastest.
Arguments:
- factors: bfloat16 [1920, 640, 640], P('aux', 'virt'), may hold values from -0.8984375 to 0.8984375
- lambda_pairs: bfloat16 [2, 640, 640], P(None, 'aux'), may hold values from -0.009765625 to 0.009765625
Outputs:
- ladder: float32 [2, 640, 3, 20], P(None, 'virt')
All inputs are finite; a program needn't handle non-finite values.
Results may differ from a plain program's by a relative error of at most 0.0027.
Values may be sent and summed in bfloat16 or wider, within the bound.
No kernel may reach another device: no remote copies, remote signals or barrier semaphores. Data moves between devices by JAX's collectives and lax.ppermute only.
A program may use at most 128 MiB of HBM per device.

v0:
```python
import jax
import jax.numpy as jnp
from jax import lax
from jax.sharding import PartitionSpec as P


def passed_along(block, axis, distance):
    devices = range(lax.axis_size(axis))
    route = [((i - distance) % len(devices), i) for i in devices]
    return lax.ppermute(block, axis, route)


def body(factors, lambda_pairs):
    lambda_full = lax.all_gather(lambda_pairs, "aux", axis=1, tiled=True)

    def make_tile(contracted):
        return jnp.einsum("pac,npbc->nab", factors, contracted, preferred_element_type=jnp.float32)

    product = jnp.einsum("pbd,ncd->npbc", factors, lambda_full, preferred_element_type=jnp.float32)
    own_part = product.astype(jnp.bfloat16)
    before = passed_along(own_part, "virt", 1)
    after = passed_along(own_part, "virt", -1)
    terms = [make_tile(before), make_tile(own_part), make_tile(after)]
    stacked = jnp.stack(terms, 2)
    return lax.psum(stacked, "aux")


def solution(mesh):
    placed = (P("aux", "virt", None), P(None, "aux", None))
    return jax.shard_map(
        body, mesh=mesh, in_specs=placed, out_specs=P(None, "virt", None, None), check_vma=False
    )
```

profile of v0, /device:TPU:4, one launch (start us, length us, event | category | flops | bytes accessed | tf_op | source)
XLA Modules:
  0.0 402.3 jit_solution(1784665801398791298)
XLA Ops:
  6.5 0.0 all-gather.2.cloned.1.call-start
  6.5 0.7 all-gather.2.cloned.1.call-update
  7.3 47.8 %all-gather.2.cloned.1.call-done = bf16[2,640,640]{2,1,0:T(8,128)(2,1)} async-done(((bf16[2,80,640]{2,1,0:T(8,128)(2,1)}), bf16[2,640,640]{2,1,0:T(8,128)(2,1)}) %all-gather.2.cloned.1.call-update) | async-done | bytes 1638416 | tf_op jit(solution)/shard_map/all_gather | solution.py:14
  55.0 15.0 %convert_bitcast_fusion = bf16[2,240,20,640]{3,1,2,0:T(8,128)(2,1)} fusion(bf16[240,20,640]{2,0,1:T(8,128)(2,1)} %param.2, bf16[2,640,640]{2,1,0:T(8,128)(2,1)} %all-gather.2.cloned.1.call-done), kind=kOutput, calls=%fused_computation.6 | convolution fusion | flops 7870464000 | bytes 20070400 | tf_op jit(solution)/shard_map/pbd,ncd->npbc/dot_general | solution.py:19
  70.0 0.0 collective-permute-start
  70.0 3.2 collective-permute-start.1
  73.3 11.4 %fusion.19 = f32[2,20,1,20]{1,3,0,2:T(8,128)S(1)} fusion(bf16[240,20,640]{2,0,1:T(8,128)(2,1)} %param.2, bf16[2,240,20,640]{3,1,2,0:T(8,128)(2,1)} %convert_bitcast_fusion), kind=kOutput, calls=%fused_computation.16 | convolution fusion | flops 245760000 | bytes 18435200 | tf_op jit(solution)/shard_map/pac,npbc->nab/dot_general | solution.py:17
  84.7 254.3 %collective-permute-done = bf16[2,240,20,640]{3,1,2,0:T(8,128)(2,1)} collective-permute-done((bf16[2,240,20,640]{3,1,2,0:T(8,128)(2,1)}, bf16[2,240,20,640]{3,1,2,0:T(8,128)(2,1)}, u32[]{:S(2)}, u32[]{:S(2)}) %collective-permute-start) | collective-permute-done | bytes 12288032 | tf_op jit(solution)/shard_map/ppermute | solution.py:10
  339.0 11.4 %fusion.14 = f32[2,20,1,20]{1,3,0,2:T(8,128)S(1)} fusion(bf16[240,20,640]{2,0,1:T(8,128)(2,1)} %param.2, bf16[2,240,20,640]{3,1,2,0:T(8,128)(2,1)} %collective-permute-done), kind=kOutput, calls=%fused_computation.15 | convolution fusion | flops 245760000 | bytes 18435200 | tf_op jit(solution)/shard_map/pac,npbc->nab/dot_general | solution.py:17
  350.4 0.0 collective-permute-done.1
  350.5 11.7 %fusion.24 = f32[2,20,1,20]{1,3,0,2:T(8,128)S(1)} fusion(bf16[240,20,640]{2,0,1:T(8,128)(2,1)} %param.2, bf16[2,240,20,640]{3,1,2,0:T(8,128)(2,1)} %collective-permute-done.1), kind=kOutput, calls=%fused_computation.17 | convolution fusion | flops 245760000 | bytes 18435200 | tf_op jit(solution)/shard_map/pac,npbc->nab/dot_general | solution.py:17
  362.1 32.6 %psum.7 = f32[2,20,3,20]{1,3,0,2:T(8,128)S(1)} all-reduce(f32[2,20,3,20]{1,3,0,2:T(8,128)S(1)} %pad_maximum_fusion), channel_id=1, replica_groups=mesh['virt'=32,'aux'=8] {'aux'}, use_global_device_ids=true, to_apply=%region_0.0 | all-reduce | flops 2400 | bytes 19200 | tf_op jit(solution)/shard_map/psum | solution.py:25
  394.7 0.7 copy.9
  (1 shorter events, 0.0 us)
Async XLA Ops:
  6.5 48.5 %all-gather.2.cloned.1.call-start = ((), (), s32[]{:S(2)}) async-start(), calls=%async_computation | async-start | bytes 1843200 | tf_op jit(solution)/shard_map/all_gather | solution.py:14
  70.0 269.0 %collective-permute-start = (bf16[2,240,20,640]{3,1,2,0:T(8,128)(2,1)}, bf16[2,240,20,640]{3,1,2,0:T(8,128)(2,1)}, u32[]{:S(2)}, u32[]{:S(2)}) collective-permute-start(bf16[2,240,20,640]{3,1,2,0:T(8,128)(2,1)} %convert_bitcast_fusion), channel_id=1, source_target_pairs={{248,0},{0,8},{8,16},{16,24},{24,32},{32,40},{40,48},{48,56},{56,6... | collective-permute-start | bytes 36864008 | tf_op jit(solution)/shard_map/ppermute | solution.py:10
  70.0 280.4 %collective-permute-start.1 = (bf16[2,240,20,640]{3,1,2,0:T(8,128)(2,1)}, bf16[2,240,20,640]{3,1,2,0:T(8,128)(2,1)}, u32[]{:S(2)}, u32[]{:S(2)}) collective-permute-start(bf16[2,240,20,640]{3,1,2,0:T(8,128)(2,1)} %convert_bitcast_fusion), channel_id=1, source_target_pairs={{8,0},{16,8},{24,16},{32,24},{40,32},{48,40},{56,48},{64,56},{72,6... | collective-permute-start | bytes 36864008 | tf_op jit(solution)/shard_map/ppermute | solution.py:10
Sparse Core Ops, SparseCore 0:
  9.1 45.8 all-gather.1
where the time goes:
time: 402 us
  waiting for transfers between devices  303 us (75%)
  matrix products  49.5 us (12%)
  blocking collectives  32.6 us (8%)
  between operations  13.4 us (3%)
    ppermute x2, waiting for transfers between devices, passed_along(): return lax.ppermute(block, axis, route)  254 us
    all_gather x1, waiting for transfers between devices, body(): lambda_full = lax.all_gather(lambda_pairs, 'aux', axis=1, tiled=True)  47.8 us
    dot_general x3, matrix products, make_tile(): jnp.einsum('pac,npbc->nab', factors, contracted, preferred_element_type=j...  34.5 us
    psum x1, blocking collectives, body(): return lax.psum(stacked, 'aux')  32.6 us
    dot_general x1, matrix products, body(): jnp.einsum('pbd,ncd->npbc', factors, lambda_full, preferred_element_type=...  15 us
  transfers between devices with their start and end apart: 3, of which 2 were waited for; matrix products, arithmetic and copies ran while one was open for 6% of the time, Pallas kernels for 0%

commit v1 on v0

v1 whole, which is shorter than its diff:
```python
import functools

import jax
import jax.numpy as jnp
from jax import lax
from jax.experimental import pallas as pl
from jax.experimental.pallas import tpu as pltpu
from jax.sharding import PartitionSpec as P

AXES = ("virt", "aux")
ROWS = 16
GROUP = 4
STEPS = 4
KEPT = 8
FREE = pl.CostEstimate(flops=1, bytes_accessed=1, transcendentals=0)
NT = (((1,), (1,)), ((), ()))
NN = (((1,), (0,)), ((), ()))


def index_of(x, y, z, core):
    return ((z % 8 * 2 + x % 4 // 2) * 2 + core) * 8 + x % 2 * 4 + y % 4


def place_of(index):
    virt, aux = divmod(index, 8)
    return virt // 2 % 2 * 2 + aux // 4, aux % 4, virt // 4, virt % 2


def route(target):
    return [(i, index_of(*target(*place_of(i)))) for i in range(256)]


def from_even(pairs):
    return [(s, t) for s, t in pairs if s // 8 % 2 == 0]


def other_core(x, y, z, core):
    return x, y, z, 1 - core


def across(x, y, z, core):
    step = 1 if core else -1
    chip = z * 2 + x // 2 + step
    return chip % 2 * 2 + x % 2, y, chip // 2 % 8, 1 - core


NEAR, FAR = route(other_core), route(across)


def send(array, pairs):
    return lax.ppermute(array, AXES, pairs)


def beside_lambda(own, core):
    half = lax.dynamic_index_in_dim(own, core, 0, keepdims=False)
    return half, send(half, route(lambda x, y, z, c: (x ^ (3 if c else 1), y, z, c)))


def gather_lambda(half, beside):
    both = jnp.stack([half, beside])

    def from_y(array, step):
        return send(array, route(lambda x, y, z, c: (x, y - step, z, c)))

    up, down = from_y(both, 1), from_y(both, -1)
    both, up, down = lax.optimization_barrier((both, up, down))
    mine = jnp.concatenate([both, up, from_y(both, 2), down])
    return mine, send(mine, NEAR)


def in_order(tile, core):
    half = tile.shape[1] // 2
    return jnp.where(core == 0, tile, jnp.concatenate([tile[:, half:], tile[:, :half]], 1))


def dot(left, right, dims):
    return lax.dot_general(left, right, dims, preferred_element_type=jnp.float32)


def folded(total, columns):
    wide = columns * ROWS
    row = lax.broadcasted_iota(jnp.int32, (ROWS, wide), 0)
    column = lax.broadcasted_iota(jnp.int32, (ROWS, wide), 1) % ROWS
    kept = jnp.where((row == column)[None], total.reshape(-1, ROWS, wide), 0.0).sum(1)
    group = lax.broadcasted_iota(jnp.int32, (wide, columns), 0) // ROWS
    ones = (group == lax.broadcasted_iota(jnp.int32, (wide, columns), 1)).astype(jnp.float32)
    return lax.dot_general(
        kept, ones, NN, precision=lax.Precision.HIGHEST, preferred_element_type=jnp.float32
    )


def side_by_side(parts):
    return jnp.concatenate(parts, 1)


def block(array, g):
    return array[:, g * ROWS : (g + 1) * ROWS].reshape(320, -1)


def own_kernel(
    place_ref, f_ref, mine_ref, theirs_ref, near_ref, sides_ref, diag_ref, near_tile_ref,
    diag, tile, lam, turned,
):
    step, core = pl.program_id(0), place_ref[0]

    @pl.when(step == 0)
    def _():
        diag[...] = jnp.zeros_like(diag)
        tile[...] = jnp.zeros_like(tile)
        for k in range(8):
            x_lo, y_at = (place_ref[1] + k % 2) % 2, (place_ref[2] + k // 2) % 4
            at = pl.ds(pl.multiple_of((x_lo * 4 + y_at) * 80, ROWS), 80)
            lam[0, at] = mine_ref[k]
            lam[1, at] = theirs_ref[k]
        for n in range(2):
            turned[:, n * 640 : (n + 1) * 640] = lam[n].T

    others = 8 * (1 - core) + jnp.where(step == 2, 0, 3)
    first = jnp.where(step < 2, 7 * core + 4 * step, others)
    at = pl.ds(pl.multiple_of(first * ROWS, ROWS), GROUP * ROWS)
    group = f_ref[:, at, :]
    rows = group.reshape(20 * GROUP * ROWS, 640)
    z = dot(rows, turned[...], NN).astype(jnp.bfloat16).reshape(20, GROUP * ROWS, 1280)

    def z_block(g):
        both = block(z, g)
        return jnp.concatenate([both[:, :640], both[:, 640:]], 0)

    z_blocks = [z_block(g) for g in range(GROUP)]
    own = [block(group, g) for g in range(GROUP)]
    own[0] = jnp.where(step == 3, jnp.zeros_like(own[0]), own[0])
    diag[...] += dot(side_by_side(own), side_by_side(z_blocks), NT)

    @pl.when(step < 2)
    def _():
        for n in range(2):
            x = dot(rows, lam[n], NN).astype(jnp.bfloat16).reshape(20, GROUP * ROWS, 640)
            for g in range(GROUP):
                sides_ref[g, n] = block(x, g)
        for g in range(GROUP):
            sides_ref[g, 2:] = z_blocks[g].reshape(2, 320, 640)
        near = near_ref[:, at, :]
        there = [block(near, g) for g in range(GROUP)]
        shared = jnp.logical_and(step == 1, core == 0)
        there[-1] = jnp.where(shared, jnp.zeros_like(there[-1]), there[-1])
        here = side_by_side([sides_ref[g].reshape(1280, 640) for g in range(GROUP)])
        tile[...] += dot(side_by_side(there), here, NT)

    @pl.when(step == STEPS - 1)
    def _():
        diag_ref[...] = folded(diag[...], 40)
        near_tile_ref[...] = folded(tile[...], 80)


def own_part(place, own, mine, theirs, near):
    whole = pl.BlockSpec(memory_space=pltpu.VMEM)
    return pl.pallas_call(
        own_kernel,
        grid_spec=pltpu.PrefetchScalarGridSpec(
            num_scalar_prefetch=1,
            grid=(STEPS,),
            in_specs=[whole] * 4,
            out_specs=[
                pl.BlockSpec((GROUP, 4, 320, 640), lambda g, c: (jnp.minimum(g, 1), 0, 0, 0)),
                pl.BlockSpec((20, 40), lambda g, c: (0, 0)),
                pl.BlockSpec((20, 80), lambda g, c: (0, 0)),
            ],
            scratch_shapes=[
                pltpu.VMEM((320, 640), jnp.float32),
                pltpu.VMEM((320, 1280), jnp.float32),
                pltpu.VMEM((2, 640, 640), jnp.bfloat16),
                pltpu.VMEM((640, 1280), jnp.bfloat16),
            ],
        ),
        out_shape=[
            jax.ShapeDtypeStruct((KEPT, 4, 320, 640), jnp.bfloat16),
            jax.ShapeDtypeStruct((20, 40), jnp.float32),
            jax.ShapeDtypeStruct((20, 80), jnp.float32),
        ],
        compiler_params=pltpu.CompilerParams(vmem_limit_bytes=60 << 20),
        cost_estimate=FREE,
        name="own_part",
    )(place, own, mine, theirs, near)


def edge_kernel(groups, *refs):
    *there_refs, tile_ref = refs
    there_refs, side_refs = there_refs[: -sum(groups)], there_refs[-sum(groups) :]
    there = [block(r, g) for r in there_refs for g in range(r.shape[1] // ROWS)]
    total, at = 0.0, 0
    for size in groups:
        here = side_by_side([r[0].reshape(1280, 640) for r in side_refs[at : at + size]])
        total = total + dot(side_by_side(there[at : at + size]), here, NT)
        at += size
    tile_ref[...] = folded(total, 80)


def edge_part(there, sides, blocks, groups):
    def side(k):
        return pl.BlockSpec((1, 4, 320, 640), lambda g: (k, 0, 0, 0))

    return pl.pallas_call(
        functools.partial(edge_kernel, groups),
        grid=(1,),
        in_specs=[pl.BlockSpec(t.shape, lambda g: (0, 0, 0)) for t in there] + [side(k) for k in blocks],
        out_specs=pl.BlockSpec((20, 80), lambda g: (0, 0)),
        out_shape=jax.ShapeDtypeStruct((20, 80), jnp.float32),
        compiler_params=pltpu.CompilerParams(vmem_limit_bytes=60 << 20),
        cost_estimate=FREE,
        name="edge_part",
    )(*there, *[sides] * len(blocks))


def flipped(tile):
    return tile.reshape(20, 2, 20).transpose(2, 1, 0).reshape(20, 40)


def body(factors, lambda_pairs):
    virt, aux = lax.axis_index("virt"), lax.axis_index("aux")
    core, x_lo, y_at = virt % 2, aux // 4, aux % 4
    own = factors.transpose(1, 0, 2)
    near = send(own, NEAR)
    half, beside = beside_lambda(lambda_pairs, core)

    def part(first, blocks):
        return lax.dynamic_slice_in_dim(own, ((1 - core) * 7 + first) * ROWS, blocks * ROWS, 1)

    last, most, rest = own[:, 14 * ROWS :], part(0, 5), part(5, 2)
    beside, last, most, rest = lax.optimization_barrier((beside, last, most, rest))
    last, most, rest = send(last, from_even(FAR)), send(most, FAR), send(rest, FAR)

    def before_far(own, near, half, beside):
        mine, theirs = gather_lambda(half, beside)
        place = jnp.stack([core, x_lo, y_at]).astype(jnp.int32)
        sides, diag, tile = own_part(place, own, mine, theirs, near)
        here, there = in_order(flipped(tile[:, :40]), core), in_order(tile[:, 40:], core)
        return sides, jnp.concatenate([in_order(diag, core), here + send(there, NEAR)], 1)

    sides, done = early(before_far, virt, own, near, half, beside)

    tile = edge_part([most, last], sides, (0, 1, 2, 3, 4, 7), (3, 3))
    tile = tile + edge_part([rest], sides, (5, 6), (2,))
    here = jnp.concatenate([in_order(flipped(tile[:, :40]), core), done], 1)
    there = in_order(tile[:, 40:], core)
    beside = lambda pairs: [(s, t ^ 4) for s, t in pairs]
    from_far = send(there, FAR) + send(there, beside(FAR))
    total = here + send(here, beside([(i, i) for i in range(256)]))
    total = total + jnp.pad(from_far, ((0, 0), (0, 80)))
    total = total + sum(lax.ppermute(total, "aux", [(a, a ^ k) for a in range(8)]) for k in (1, 2, 3))
    far_tile, diag, near_tile = [total[:, i * 40 : i * 40 + 40].reshape(20, 2, 20) for i in range(3)]
    before = jnp.where(core == 0, far_tile, near_tile)
    after = jnp.where(core == 0, near_tile, far_tile)
    return jnp.stack([before, diag, after], 2).transpose(1, 0, 2, 3)


def early(part, virt, *operands):
    def nothing(*operands):
        shapes = jax.eval_shape(part, *operands)
        return jax.tree.map(lambda s: jnp.zeros(s.shape, s.dtype), shapes)

    return lax.cond(virt < lax.axis_size("virt"), part, nothing, *operands)


def solution(mesh):
    placed = (P("aux", "virt", None), P(None, "aux", None))
    return jax.shard_map(
        body, mesh=mesh, in_specs=placed, out_specs=P(None, "virt", None, None), check_vma=False
    )
```

time: 402 us -> 118 us (0.29)
  the two profiles are of different devices: /device:TPU:4 before, /device:TPU:24 now
where the time goes in v1:
time: 118 us; the launch traced here: 117 us
  Pallas kernels  50.9 us (43%)
  starting transfers between devices  32.7 us (28%)
  waiting for transfers between devices  18.1 us (15%)
  local copies, waits for them, and re-layouts  11.2 us (9%)
  other arithmetic  4.18 us (4%)
    pallas_call x1, Pallas kernels, own_part(): pl.pallas_call(own_kernel, grid_spec=pltpu.PrefetchScalarGridSpec(num_sca...  37.3 us
    ppermute x13, starting transfers between devices, send(): return lax.ppermute(array, AXES, pairs)  28 us
    pallas_call x2, Pallas kernels, edge_part(): pl.pallas_call(functools.partial(edge_kernel, groups), grid=(1,), in_spec...  13.6 us
    ppermute x13, waiting for transfers between devices, send(): return lax.ppermute(array, AXES, pairs)  13.2 us
    dynamic_slice x2, local copies, waits for them, and re-layouts, part(): lax.dynamic_slice_in_dim(own, ((1 - core) * 7 + first) * ROWS, blocks * R...  5.2 us
    ppermute x3, waiting for transfers between devices, body(): lax.ppermute(total, 'aux', [(a, a ^ k) for a in range(8)])  4.9 us
    ppermute x3, starting transfers between devices, body(): lax.ppermute(total, 'aux', [(a, a ^ k) for a in range(8)])  4.73 us
  transfers between devices with their start and end apart: 16, of which 8 were waited for; matrix products, arithmetic and copies ran while one was open for 9% of the time, Pallas kernels for 36%

profile of v1, /device:TPU:24, one launch (start us, length us, event | category | flops | bytes accessed | tf_op | source)
XLA Modules:
  0.0 117.4 jit_solution(8103014770180996769)
XLA Ops:
  0.0 0.9 copy-done
  0.9 1.6 %collective-permute-start.5 = (bf16[80,640]{1,0:T(8,128)(2,1)S(1)}, bf16[80,640]{1,0:T(8,128)(2,1)S(1)}, u32[]{:S(2)}, u32[]{:S(2)}) collective-permute-start(bf16[80,640]{1,0:T(8,128)(2,1)S(1)} %dynamic-slice_bitcast_fusion.2), channel_id=1, source_target_pairs={{0,4},{1,5},{2,6},{3,7},{4,0},{5,1},{6,2},{7,3},{8,28},{9,29},{10,... | collective-permute-start | bytes 307208 | tf_op jit(solution)/shard_map/ppermute | solution.py:51
  2.5 1.0 slice.70
  3.6 3.1 %dynamic-slice_bitcast_fusion = bf16[20,80,640]{2,1,0:T(8,128)(2,1)} fusion(bf16[240,20,640]{2,0,1:T(8,128)(2,1)} %param.4, s32[]{:T(128)S(6)} %select_n.86), kind=kLoop, calls=%fused_computation.11 | loop fusion | bytes 4096004 | tf_op jit(solution)/shard_map/dynamic_slice | solution.py:226
  6.6 2.1 %dynamic-slice_bitcast_fusion.1 = bf16[20,32,640]{2,1,0:T(8,128)(2,1)} fusion(bf16[240,20,640]{2,0,1:T(8,128)(2,1)} %param.4, s32[]{:T(128)S(6)} %select_n.87), kind=kLoop, calls=%fused_computation.12 | loop fusion | bytes 1638404 | tf_op jit(solution)/shard_map/dynamic_slice | solution.py:226
  8.8 6.5 %collective-permute-start.6 = (bf16[20,80,640]{2,1,0:T(8,128)(2,1)}, bf16[20,80,640]{2,1,0:T(8,128)(2,1)S(1)}, u32[]{:S(2)}, u32[]{:S(2)}) collective-permute-start(bf16[20,80,640]{2,1,0:T(8,128)(2,1)} %dynamic-slice_bitcast_fusion), channel_id=1, source_target_pairs={{0,248},{1,249},{2,250},{3,251},{4,252},{5,253},{6,254},{7,255},{8... | collective-permute-start | bytes 6144008 | tf_op jit(solution)/shard_map/ppermute | solution.py:51
  15.3 8.0 %collective-permute-start.7 = (bf16[20,16,640]{2,1,0:T(8,128)(2,1)S(1)}, bf16[20,16,640]{2,1,0:T(8,128)(2,1)}, u32[]{:S(2)}, u32[]{:S(2)}) collective-permute-start(bf16[20,16,640]{2,1,0:T(8,128)(2,1)S(1)} %slice.70), channel_id=1, source_target_pairs={{0,248},{1,249},{2,250},{3,251},{4,252},{5,253},{6,254},{7,255},{1... | collective-permute-start | bytes 1228808 | tf_op jit(solution)/shard_map/ppermute | solution.py:51
  23.4 58.9 %conditional.1 = (bf16[8,4,320,640]{3,2,1,0:T(8,128)(2,1)}, f32[20,80]{1,0:T(8,128)S(1)}) conditional(s32[]{:T(128)} %convert_element_type.5, () %tuple.29, (s32[]{:T(128)}, s32[]{:T(128)}, s32[]{:T(128)}, bf16[80,640]{1,0:T(8,128)(2,1)S(1)}, bf16[80,640]{1,0:T(8,128)(2,1)S(1)}, /*index=5*/bf16[20,240,640]{2,1,0:T(8,128)(2,1)}, ...), branch_computations={%region_0.1_spmd, %region_1.2_spmd} | conditional | flops 109627 | bytes 13113622 | solution.py:261
  24.2 2.5 %collective-permute-start.1 = (bf16[2,80,640]{2,1,0:T(8,128)(2,1)S(1)}, bf16[2,80,640]{2,1,0:T(8,128)(2,1)S(1)}, u32[]{:S(2)}, u32[]{:S(2)}) collective-permute-start(bf16[2,80,640]{2,1,0:T(8,128)(2,1)S(1)} %pad_maximum_fusion), channel_id=1, source_target_pairs={{0,1},{1,2},{2,3},{3,0},{4,5},{5,6},{6,7},{7,4},{8,9},{9,10},{10,1... | collective-permute-start | bytes 614408 | tf_op jit(solution)/shard_map/cond/branch_1_fun/ppermute | solution.py:51
  26.7 3.7 %collective-permute-done = bf16[2,80,640]{2,1,0:T(8,128)(2,1)S(1)} collective-permute-done((bf16[2,80,640]{2,1,0:T(8,128)(2,1)S(1)}, bf16[2,80,640]{2,1,0:T(8,128)(2,1)S(1)}, u32[]{:S(2)}, u32[]{:S(2)}) %collective-permute-start) | collective-permute-done | bytes 204832 | tf_op jit(solution)/shard_map/cond/branch_1_fun/ppermute | solution.py:51
  30.4 1.5 %collective-permute-start.2 = (bf16[2,80,640]{2,1,0:T(8,128)(2,1)S(1)}, bf16[2,80,640]{2,1,0:T(8,128)(2,1)S(1)}, u32[]{:S(2)}, u32[]{:S(2)}) collective-permute-start(bf16[2,80,640]{2,1,0:T(8,128)(2,1)S(1)} %pad_maximum_fusion), channel_id=1, source_target_pairs={{0,2},{1,3},{2,0},{3,1},{4,6},{5,7},{6,4},{7,5},{8,10},{9,11},{10,... | collective-permute-start | bytes 614408 | tf_op jit(solution)/shard_map/cond/branch_1_fun/ppermute | solution.py:51
  32.0 5.7 %collective-permute-done.2 = bf16[2,80,640]{2,1,0:T(8,128)(2,1)S(1)} collective-permute-done((bf16[2,80,640]{2,1,0:T(8,128)(2,1)S(1)}, bf16[2,80,640]{2,1,0:T(8,128)(2,1)S(1)}, u32[]{:S(2)}, u32[]{:S(2)}) %collective-permute-start.2) | collective-permute-done | bytes 204832 | tf_op jit(solution)/shard_map/cond/branch_1_fun/ppermute | solution.py:51
  38.7 1.8 %collective-permute-done.3.theirs_ref = bf16[8,80,640]{2,1,0:T(8,128)(2,1)} collective-permute-done((bf16[8,80,640]{2,1,0:T(8,128)(2,1)S(1)}, bf16[8,80,640]{2,1,0:T(8,128)(2,1)}, u32[]{:S(2)}, u32[]{:S(2)}) %collective-permute-start.3) | collective-permute-done | bytes 819232 | tf_op jit(solution)/shard_map/cond/branch_1_fun/ppermute | solution.py:51
  40.5 37.3 %own_part.1 = (bf16[8,4,320,640]{3,2,1,0:T(8,128)(2,1)}, f32[20,40]{1,0:T(8,128)}, f32[20,80]{1,0:T(8,128)}) custom-call(s32[3]{0:T(128)} %pad_add_fusion.place_ref, bf16[20,240,640]{2,1,0:T(8,128)(2,1)} %get-tuple-element.65.f_ref, bf16[8,80,640]{2,1,0:T(8,128)(2,1)} %copy-done.2, bf16[8,80,640]{2,1,0:T(8,128)(2,1)} %collective-permute-done.3.theirs_ref, ...), custom_call_target="tpu_custom_call" | custom-call | flops 1 | bytes 1 | tf_op jit(solution)/shard_map/cond/branch_1_fun/own_part/pallas_call | solution.py:157
  77.8 0.9 fusion.1
  78.6 0.9 fusion.4
  79.5 0.9 fusion.3
  82.3 4.4 %edge_part.3 = f32[20,80]{1,0:T(8,128)} custom-call(bf16[20,32,640]{2,1,0:T(8,128)(2,1)} %collective-permute-done.9.refs_0_, bf16[8,4,320,640]{3,2,1,0:T(8,128)(2,1)} %get-tuple-element.84.refs_2_.refs_3_.refs_4_.refs_5_.refs_6_.refs_7_.refs_1_, bf16[8,4,320,640]{3,2,1,0:T(8,128)(2,1)} %get-tuple-element.84.refs_2_.refs_3_.refs_4_.refs_5_.refs_6_.refs_7_.refs_1_), custom_call_target="tpu_custom_call" | custom-call | flops 1 | bytes 1 | tf_op jit(solution)/shard_map/edge_part/pallas_call | solution.py:202
  86.7 1.3 %copy-done.1 = bf16[20,80,640]{2,1,0:T(8,128)(2,1)} copy-done((bf16[20,80,640]{2,1,0:T(8,128)(2,1)}, bf16[20,80,640]{2,1,0:T(8,128)(2,1)S(1)}, u32[]{:S(2)}) %copy-start.1) | copy-done | bytes 2048024
  88.0 9.2 %edge_part.2 = f32[20,80]{1,0:T(8,128)} custom-call(bf16[20,80,640]{2,1,0:T(8,128)(2,1)} %copy-done.1, bf16[20,16,640]{2,1,0:T(8,128)(2,1)} %collective-permute-done.7.refs_1_, bf16[8,4,320,640]{3,2,1,0:T(8,128)(2,1)} %get-tuple-element.84.refs_2_.refs_3_.refs_4_.refs_5_.refs_6_.refs_7_.refs_1_, ...), custom_call_target="tpu_custom_call" | custom-call | flops 1 | bytes 1 | tf_op jit(solution)/shard_map/edge_part/pallas_call | solution.py:202
  99.6 5.6 %collective-permute-start.12 = (f32[20,40]{1,0:T(8,128)S(1)}, f32[20,40]{1,0:T(8,128)S(1)}, u32[]{:S(2)}, u32[]{:S(2)}) collective-permute-start(f32[20,40]{1,0:T(8,128)S(1)} %get-tuple-element.103), channel_id=1, source_target_pairs={{0,252},{1,253},{2,254},{3,255},{4,248},{5,249},{6,250},{7,251},{8... | collective-permute-start | bytes 9608 | tf_op jit(solution)/shard_map/ppermute | solution.py:51
  107.3 4.1 %collective-permute-start.14 = (f32[20,120]{1,0:T(8,128)S(1)}, f32[20,120]{1,0:T(8,128)S(1)}, u32[]{:S(2)}, u32[]{:S(2)}) collective-permute-start(f32[20,120]{1,0:T(8,128)S(1)} %pad_add_fusion.1), channel_id=1, source_target_pairs={{0,2},{1,3},{2,0},{3,1},{4,6},{5,7},{6,4},{7,5},{8,10},{9,11},{10,... | collective-permute-start | bytes 28808 | tf_op jit(solution)/shard_map/ppermute | solution.py:249
  111.5 1.8 %collective-permute-done.14 = f32[20,120]{1,0:T(8,128)S(1)} collective-permute-done((f32[20,120]{1,0:T(8,128)S(1)}, f32[20,120]{1,0:T(8,128)S(1)}, u32[]{:S(2)}, u32[]{:S(2)}) %collective-permute-start.14) | collective-permute-done | bytes 9632 | tf_op jit(solution)/shard_map/ppermute | solution.py:249
  113.3 3.1 %collective-permute-done.15 = f32[20,120]{1,0:T(8,128)S(1)} collective-permute-done((f32[20,120]{1,0:T(8,128)S(1)}, f32[20,120]{1,0:T(8,128)S(1)}, u32[]{:S(2)}, u32[]{:S(2)}) %collective-permute-start.15) | collective-permute-done | bytes 9632 | tf_op jit(solution)/shard_map/ppermute | solution.py:249
  (57 shorter events, 9.3 us)
Async XLA Ops:
  0.0 0.9 copy-start
  0.0 23.4 %collective-permute-start.8 = (bf16[20,240,640]{2,1,0:T(8,128)(2,1)}, bf16[20,240,640]{2,1,0:T(8,128)(2,1)}, u32[]{:S(2)}, u32[]{:S(2)}) collective-permute-start(bf16[20,240,640]{2,1,0:T(8,128)(2,1)} %bitcast.19), channel_id=1, source_target_pairs={{0,8},{1,9},{2,10},{3,11},{4,12},{5,13},{6,14},{7,15},{8,0},{9,1},... | collective-permute-start | bytes 18432008 | tf_op jit(solution)/shard_map/ppermute | solution.py:51
  0.9 7.8 %collective-permute-start.5 = (bf16[80,640]{1,0:T(8,128)(2,1)S(1)}, bf16[80,640]{1,0:T(8,128)(2,1)S(1)}, u32[]{:S(2)}, u32[]{:S(2)}) collective-permute-start(bf16[80,640]{1,0:T(8,128)(2,1)S(1)} %dynamic-slice_bitcast_fusion.2), channel_id=1, source_target_pairs={{0,4},{1,5},{2,6},{3,7},{4,0},{5,1},{6,2},{7,3},{8,28},{9,29},{10,... | collective-permute-start | bytes 307208 | tf_op jit(solution)/shard_map/ppermute | solution.py:51
  8.8 77.9 %collective-permute-start.6 = (bf16[20,80,640]{2,1,0:T(8,128)(2,1)}, bf16[20,80,640]{2,1,0:T(8,128)(2,1)S(1)}, u32[]{:S(2)}, u32[]{:S(2)}) collective-permute-start(bf16[20,80,640]{2,1,0:T(8,128)(2,1)} %dynamic-slice_bitcast_fusion), channel_id=1, source_target_pairs={{0,248},{1,249},{2,250},{3,251},{4,252},{5,253},{6,254},{7,255},{8... | collective-permute-start | bytes 6144008 | tf_op jit(solution)/shard_map/ppermute | solution.py:51
  15.3 67.0 %collective-permute-start.9 = (bf16[20,32,640]{2,1,0:T(8,128)(2,1)}, bf16[20,32,640]{2,1,0:T(8,128)(2,1)}, u32[]{:S(2)}, u32[]{:S(2)}) collective-permute-start(bf16[20,32,640]{2,1,0:T(8,128)(2,1)} %dynamic-slice_bitcast_fusion.1), channel_id=1, source_target_pairs={{0,248},{1,249},{2,250},{3,251},{4,252},{5,253},{6,254},{7,255},{8... | collective-permute-start | bytes 2457608 | tf_op jit(solution)/shard_map/ppermute | solution.py:51
  15.3 71.4 %collective-permute-start.7 = (bf16[20,16,640]{2,1,0:T(8,128)(2,1)S(1)}, bf16[20,16,640]{2,1,0:T(8,128)(2,1)}, u32[]{:S(2)}, u32[]{:S(2)}) collective-permute-start(bf16[20,16,640]{2,1,0:T(8,128)(2,1)S(1)} %slice.70), channel_id=1, source_target_pairs={{0,248},{1,249},{2,250},{3,251},{4,252},{5,253},{6,254},{7,255},{1... | collective-permute-start | bytes 1228808 | tf_op jit(solution)/shard_map/ppermute | solution.py:51
  23.4 7.0 %collective-permute-start = (bf16[2,80,640]{2,1,0:T(8,128)(2,1)S(1)}, bf16[2,80,640]{2,1,0:T(8,128)(2,1)S(1)}, u32[]{:S(2)}, u32[]{:S(2)}) collective-permute-start(bf16[2,80,640]{2,1,0:T(8,128)(2,1)S(1)} %pad_maximum_fusion), channel_id=1, source_target_pairs={{0,3},{1,0},{2,1},{3,2},{4,7},{5,4},{6,5},{7,6},{8,11},{9,8},{10,9... | collective-permute-start | bytes 614408 | tf_op jit(solution)/shard_map/cond/branch_1_fun/ppermute | solution.py:51
  24.2 6.2 %collective-permute-start.1 = (bf16[2,80,640]{2,1,0:T(8,128)(2,1)S(1)}, bf16[2,80,640]{2,1,0:T(8,128)(2,1)S(1)}, u32[]{:S(2)}, u32[]{:S(2)}) collective-permute-start(bf16[2,80,640]{2,1,0:T(8,128)(2,1)S(1)} %pad_maximum_fusion), channel_id=1, source_target_pairs={{0,1},{1,2},{2,3},{3,0},{4,5},{5,6},{6,7},{7,4},{8,9},{9,10},{10,1... | collective-permute-start | bytes 614408 | tf_op jit(solution)/shard_map/cond/branch_1_fun/ppermute | solution.py:51
  30.4 7.3 %collective-permute-start.2 = (bf16[2,80,640]{2,1,0:T(8,128)(2,1)S(1)}, bf16[2,80,640]{2,1,0:T(8,128)(2,1)S(1)}, u32[]{:S(2)}, u32[]{:S(2)}) collective-permute-start(bf16[2,80,640]{2,1,0:T(8,128)(2,1)S(1)} %pad_maximum_fusion), channel_id=1, source_target_pairs={{0,2},{1,3},{2,0},{3,1},{4,6},{5,7},{6,4},{7,5},{8,10},{9,11},{10,... | collective-permute-start | bytes 614408 | tf_op jit(solution)/shard_map/cond/branch_1_fun/ppermute | solution.py:51
  37.8 2.7 %copy-start.2 = (bf16[8,80,640]{2,1,0:T(8,128)(2,1)}, bf16[8,80,640]{2,1,0:T(8,128)(2,1)S(1)}, u32[]{:S(2)}) copy-start(bf16[8,80,640]{2,1,0:T(8,128)(2,1)S(1)} %constant_dynamic-update-slice_fusion.mine_ref) | copy-start | bytes 2457604 | tf_op jit(solution)/shard_map/cond
  37.8 2.7 %collective-permute-start.3 = (bf16[8,80,640]{2,1,0:T(8,128)(2,1)S(1)}, bf16[8,80,640]{2,1,0:T(8,128)(2,1)}, u32[]{:S(2)}, u32[]{:S(2)}) collective-permute-start(bf16[8,80,640]{2,1,0:T(8,128)(2,1)S(1)} %constant_dynamic-update-slice_fusion.mine_ref), channel_id=1, source_target_pairs={{0,8},{1,9},{2,10},{3,11},{4,12},{5,13},{6,14},{7,15},{8,0},{9,1},... | collective-permute-start | bytes 2457608 | tf_op jit(solution)/shard_map/cond/branch_1_fun/ppermute | solution.py:51
  80.7 1.4 %collective-permute-start.4 = (f32[20,40]{1,0:T(8,128)S(1)}, f32[20,40]{1,0:T(8,128)S(1)}, u32[]{:S(2)}, u32[]{:S(2)}) collective-permute-start(f32[20,40]{1,0:T(8,128)S(1)} %get-tuple-element.94), channel_id=1, source_target_pairs={{0,8},{1,9},{2,10},{3,11},{4,12},{5,13},{6,14},{7,15},{8,0},{9,1},... | collective-permute-start | bytes 9608 | tf_op jit(solution)/shard_map/cond/branch_1_fun/ppermute | solution.py:51
  86.7 10.5 %copy-start.3 = (f32[20,80]{1,0:T(8,128)S(1)}, f32[20,80]{1,0:T(8,128)}, u32[]{:S(2)}) copy-start(f32[20,80]{1,0:T(8,128)} %edge_part.3) | copy-start | bytes 19204
  86.7 1.3 %copy-start.1 = (bf16[20,80,640]{2,1,0:T(8,128)(2,1)}, bf16[20,80,640]{2,1,0:T(8,128)(2,1)S(1)}, u32[]{:S(2)}) copy-start(bf16[20,80,640]{2,1,0:T(8,128)(2,1)S(1)} %collective-permute-done.6.refs_0_) | copy-start | bytes 6144004
  98.6 8.1 %collective-permute-start.10 = (f32[20,120]{1,0:T(8,128)S(1)}, f32[20,120]{1,0:T(8,128)S(1)}, u32[]{:S(2)}, u32[]{:S(2)}) collective-permute-start(f32[20,120]{1,0:T(8,128)S(1)} %pad_maximum_fusion.2), channel_id=1, source_target_pairs={{0,4},{1,5},{2,6},{3,7},{4,0},{5,1},{6,2},{7,3},{8,12},{9,13},{10,... | collective-permute-start | bytes 28808 | tf_op jit(solution)/shard_map/ppermute | solution.py:51
  99.1 6.7 %collective-permute-start.11 = (f32[20,40]{1,0:T(8,128)S(1)}, f32[20,40]{1,0:T(8,128)S(1)}, u32[]{:S(2)}, u32[]{:S(2)}) collective-permute-start(f32[20,40]{1,0:T(8,128)S(1)} %get-tuple-element.103), channel_id=1, source_target_pairs={{0,248},{1,249},{2,250},{3,251},{4,252},{5,253},{6,254},{7,255},{8... | collective-permute-start | bytes 9608 | tf_op jit(solution)/shard_map/ppermute | solution.py:51
  99.6 7.1 %collective-permute-start.12 = (f32[20,40]{1,0:T(8,128)S(1)}, f32[20,40]{1,0:T(8,128)S(1)}, u32[]{:S(2)}, u32[]{:S(2)}) collective-permute-start(f32[20,40]{1,0:T(8,128)S(1)} %get-tuple-element.103), channel_id=1, source_target_pairs={{0,252},{1,253},{2,254},{3,255},{4,248},{5,249},{6,250},{7,251},{8... | collective-permute-start | bytes 9608 | tf_op jit(solution)/shard_map/ppermute | solution.py:51
  106.7 4.7 %collective-permute-start.13 = (f32[20,120]{1,0:T(8,128)S(1)}, f32[20,120]{1,0:T(8,128)S(1)}, u32[]{:S(2)}, u32[]{:S(2)}) collective-permute-start(f32[20,120]{1,0:T(8,128)S(1)} %pad_add_fusion.1), channel_id=1, source_target_pairs={{0,1},{1,0},{2,3},{3,2},{4,5},{5,4},{6,7},{7,6},{8,9},{9,8},{10,11... | collective-permute-start | bytes 28808 | tf_op jit(solution)/shard_map/ppermute | solution.py:249
  107.3 5.9 %collective-permute-start.14 = (f32[20,120]{1,0:T(8,128)S(1)}, f32[20,120]{1,0:T(8,128)S(1)}, u32[]{:S(2)}, u32[]{:S(2)}) collective-permute-start(f32[20,120]{1,0:T(8,128)S(1)} %pad_add_fusion.1), channel_id=1, source_target_pairs={{0,2},{1,3},{2,0},{3,1},{4,6},{5,7},{6,4},{7,5},{8,10},{9,11},{10,... | collective-permute-start | bytes 28808 | tf_op jit(solution)/shard_map/ppermute | solution.py:249
  111.5 4.9 %collective-permute-start.15 = (f32[20,120]{1,0:T(8,128)S(1)}, f32[20,120]{1,0:T(8,128)S(1)}, u32[]{:S(2)}, u32[]{:S(2)}) collective-permute-start(f32[20,120]{1,0:T(8,128)S(1)} %pad_add_fusion.1), channel_id=1, source_target_pairs={{0,3},{1,2},{2,1},{3,0},{4,7},{5,6},{6,5},{7,4},{8,11},{9,10},{10,... | collective-permute-start | bytes 28808 | tf_op jit(solution)/shard_map/ppermute | solution.py:249

commit v2 on v0

v2 whole, which is shorter than its diff:
```python
import functools

import jax
import jax.numpy as jnp
from jax import lax
from jax.experimental import pallas as pl
from jax.experimental.pallas import tpu as pltpu
from jax.sharding import PartitionSpec as P

AXES = ("virt", "aux")
ROWS = 16
KEPT = 8
FREE = pl.CostEstimate(flops=1, bytes_accessed=1, transcendentals=0)
NT = (((1,), (1,)), ((), ()))
NN = (((1,), (0,)), ((), ()))


def index_of(x, y, z, core):
    return ((z % 8 * 2 + x % 4 // 2) * 2 + core) * 8 + x % 2 * 4 + y % 4


def place_of(index):
    virt, aux = divmod(index, 8)
    return virt // 2 % 2 * 2 + aux // 4, aux % 4, virt // 4, virt % 2


def route(target):
    return [(i, index_of(*target(*place_of(i)))) for i in range(256)]


def from_even(pairs):
    return [(s, t) for s, t in pairs if s // 8 % 2 == 0]


def other_core(x, y, z, core):
    return x, y, z, 1 - core


def across(x, y, z, core):
    step = 1 if core else -1
    chip = z * 2 + x // 2 + step
    return chip % 2 * 2 + x % 2, y, chip // 2 % 8, 1 - core


NEAR, FAR, HERE = route(other_core), route(across), [(i, i) for i in range(256)]


def send(array, pairs):
    return lax.ppermute(array, AXES, pairs)


def beside_lambda(own, core):
    half = lax.dynamic_index_in_dim(own, core, 0, keepdims=False)
    return half, send(half, route(lambda x, y, z, c: (x ^ (3 if c else 1), y, z, c)))


def dot(left, right, dims):
    return lax.dot_general(left, right, dims, preferred_element_type=jnp.float32)


def folded(total, core):
    wide = total.shape[1]
    columns = wide // ROWS
    row = lax.broadcasted_iota(jnp.int32, (ROWS, wide), 0)
    column = lax.broadcasted_iota(jnp.int32, (ROWS, wide), 1) % ROWS
    kept = jnp.where((row == column)[None], total.reshape(-1, ROWS, wide), 0.0).sum(1)
    group = lax.broadcasted_iota(jnp.int32, (wide, columns), 0) // ROWS
    place = group // 40 * 40 + (group + 20 * core) % 40
    ones = (place == lax.broadcasted_iota(jnp.int32, (wide, columns), 1)).astype(jnp.float32)
    return lax.dot_general(
        kept, ones, NN, precision=lax.Precision.HIGHEST, preferred_element_type=jnp.float32
    )


def side_by_side(parts):
    return jnp.concatenate(parts, 1)


def block(array, g):
    return array[:, g * ROWS : (g + 1) * ROWS].reshape(320, -1)


def own_kernel(
    place_ref, f_hbm, *refs
):
    lam_refs, (sides_hbm, diag_ref, f_buf, sides, rows_cd, cols_cd, f_sem, sides_sem) = refs[:8], refs[8:]
    core = place_ref[0]
    firsts = (7 * core, 7 * core + 4, 8 * (1 - core), 8 * (1 - core) + 4)
    sizes = (4, 4, 4, 3)

    def copied(step):
        count = sizes[step] * ROWS
        rows = pl.ds(pl.multiple_of(firsts[step] * ROWS, ROWS), count)
        return pltpu.make_async_copy(
            f_hbm.at[:, rows, :], f_buf.at[step, :, pl.ds(0, count), :], f_sem.at[step]
        )

    f_copies = [copied(step) for step in range(4)]
    side_copies = [
        pltpu.make_async_copy(sides.at[pair], sides_hbm.at[pair], sides_sem.at[pair]) for pair in range(4)
    ]
    for copy in f_copies:
        copy.start()

    for k in range(8):
        x_lo, y_at = place_ref[1] ^ (k % 2), (place_ref[2] + k // 2) % 4
        at = pl.ds(pl.multiple_of((x_lo * 4 + y_at) * 80, ROWS), 80)
        for n in range(2):
            part = lam_refs[4 * n + k // 2][k % 2]
            rows_cd[n, at] = part
            cols_cd[at, 640 * n : 640 * n + 640] = part

    diag = 0.0
    for step, size in enumerate(sizes):
        f_copies[step].wait()
        group = f_buf[step, :, : size * ROWS]
        rows = group.reshape(20 * size * ROWS, 640)
        first = 2 * min(step, 2)

        def keep(product, q):
            product = product.astype(jnp.bfloat16).reshape(20, size * ROWS, 1280)
            for n in range(2):
                for g in range(size):
                    part = product[:, g * ROWS : (g + 1) * ROWS, 640 * n : 640 * n + 640].reshape(320, 640)
                    at = (first + g // 2, slice(320 * (q + n), 320 * (q + n) + 320), pl.ds(640 * (g % 2), 640))
                    sides[at] = part

        keep(dot(rows, rows_cd[...].reshape(1280, 640), NT), 2)
        if step < 2:
            keep(dot(rows, cols_cd[...], NN), 0)
            for copy in side_copies[first : first + 2]:
                copy.start()
        for g in range(0, size, 2):
            count = min(2, size - g)
            own = side_by_side([block(group, g + k) for k in range(count)])
            diag = diag + dot(own, sides[first + g // 2, 640:, : 640 * count], NT)

    diag_ref[...] = folded(diag, core)
    for copy in side_copies:
        copy.wait()


def own_part(place, own, mine, theirs):
    vmem, hbm = pl.BlockSpec(memory_space=pltpu.VMEM), pl.BlockSpec(memory_space=pl.ANY)
    return pl.pallas_call(
        own_kernel,
        in_specs=[pl.BlockSpec(memory_space=pltpu.SMEM), hbm] + [vmem] * 8,
        out_specs=[hbm, vmem],
        scratch_shapes=[
            pltpu.VMEM((4, 20, 4 * ROWS, 640), jnp.bfloat16),
            pltpu.VMEM((6, 1280, 1280), jnp.bfloat16),
            pltpu.VMEM((2, 640, 640), jnp.bfloat16),
            pltpu.VMEM((640, 1280), jnp.bfloat16),
            pltpu.SemaphoreType.DMA((4,)),
            pltpu.SemaphoreType.DMA((4,)),
        ],
        out_shape=[
            jax.ShapeDtypeStruct((4, 1280, 1280), jnp.bfloat16),
            jax.ShapeDtypeStruct((20, 40), jnp.float32),
        ],
        compiler_params=pltpu.CompilerParams(vmem_limit_bytes=44 << 20),
        cost_estimate=FREE,
        name="own_part",
    )(place, own, *mine, *theirs)


def edge_kernel(place_ref, *refs):
    there_refs, (sides_ref, here_ref, back_ref, total) = refs[:-4], refs[-4:]
    step, core = pl.program_id(0), place_ref[0]
    there = [r[...].reshape(320, 640) for r in there_refs[:2]]
    none = jnp.zeros_like(there[0])
    if len(there_refs) == 3:
        there[0] = jnp.where(step == 3, none, there[0])
        there[1] = jnp.where(step == 3, there_refs[2][...].reshape(320, 640), there[1])
    else:
        there[1] = jnp.where(jnp.logical_and(step == 3, core == 0), none, there[1])
    product = dot(side_by_side(there), sides_ref[0], NT)

    @pl.when(step == 0)
    def _():
        total[...] = product

    @pl.when(jnp.logical_and(step > 0, step < 3))
    def _():
        total[...] += product

    @pl.when(step == 3)
    def _():
        tile = folded(total[...] + product, core)
        here_ref[...] = tile[:, :40]
        back_ref[...] = tile[:, 40:]


def edge_part(place, there, sides):
    def rows(at):
        return pl.BlockSpec((20, ROWS, 640), lambda g, p: (0, at(g, p), 0))

    if len(there) == 1:
        specs = [rows(lambda g, p, k=k: 7 * p[0] + 2 * g + k) for k in range(2)]
    else:
        specs = [rows(lambda g, p, k=k: jnp.minimum(2 * g + k, 5)) for k in range(2)] + [rows(lambda g, p: 0)]
    return pl.pallas_call(
        edge_kernel,
        grid_spec=pltpu.PrefetchScalarGridSpec(
            num_scalar_prefetch=1,
            grid=(4,),
            in_specs=specs + [pl.BlockSpec((1, 1280, 1280), lambda g, p: (g, 0, 0))],
            out_specs=[pl.BlockSpec((20, 40), lambda g, p: (0, 0))] * 2,
            scratch_shapes=[pltpu.VMEM((320, 1280), jnp.float32)],
        ),
        out_shape=[jax.ShapeDtypeStruct((20, 40), jnp.float32)] * 2,
        compiler_params=pltpu.CompilerParams(vmem_limit_bytes=24 << 20),
        cost_estimate=FREE,
        name="edge_part",
    )(place, *[there[0]] * 2, *there[1:], sides)


def last_kernel(place_ref, here_ref, back_ref, diag_ref, near_ref, from_near_ref, rest_ref, side_ref, mine_ref, there_ref):
    tile = folded(dot(rest_ref[...].reshape(320, 640), side_ref[0], NT), place_ref[0])
    mine_ref[0] = here_ref[...] + tile[:, :40]
    mine_ref[1] = diag_ref[...]
    mine_ref[2] = near_ref[...]
    mine_ref[3] = from_near_ref[...]
    there_ref[...] = back_ref[...] + tile[:, 40:]


def last_part(place, small, rest, sides):
    def whole(*shape):
        return pl.BlockSpec(shape, lambda g: (0,) * len(shape))

    return pl.pallas_call(
        last_kernel,
        grid=(1,),
        in_specs=[pl.BlockSpec(memory_space=pltpu.SMEM)]
        + [whole(20, 40)] * len(small)
        + [whole(20, ROWS, 640), pl.BlockSpec((1, 1280, 640), lambda g: (3, 0, 0))],
        out_specs=[whole(4, 20, 40), whole(20, 40)],
        out_shape=[jax.ShapeDtypeStruct(shape, jnp.float32) for shape in ((4, 20, 40), (20, 40))],
        compiler_params=pltpu.CompilerParams(vmem_limit_bytes=16 << 20),
        cost_estimate=FREE,
        name="last_part",
    )(place, *small, rest, sides)


def flipped(tile):
    return tile.reshape(20, 2, 20).transpose(2, 1, 0).reshape(20, 40)


def body(factors, lambda_pairs):
    virt, aux = lax.axis_index("virt"), lax.axis_index("aux")
    core = virt % 2
    place = jnp.stack([core, aux // 4, aux % 4]).astype(jnp.int32)
    own = factors.transpose(1, 0, 2)
    half, beside = beside_lambda(lambda_pairs, core)

    def part(first, blocks):
        return lax.dynamic_slice_in_dim(own, ((1 - core) * 7 + first) * ROWS, blocks * ROWS, 1)

    most = part(0, 6)
    beside, most = lax.optimization_barrier((beside, most))
    most = send(most, FAR)
    both = jnp.stack([half, beside])
    ring = [both] + [send(both, route(lambda x, y, z, c, k=k: (x, y - k, z, c))) for k in (1, 2, 3)]
    ring, last, rest = lax.optimization_barrier((ring, own[:, 14 * ROWS :], part(6, 1)))
    last, rest = send(last, from_even(FAR)), send(rest, FAR)

    def before_far(own, *mine):
        theirs = [send(m, NEAR) for m in mine[:2]]
        theirs, *after = lax.optimization_barrier((theirs, *mine[2:]))
        theirs, near = lax.optimization_barrier((theirs + [send(m, NEAR) for m in after], own))
        near = send(near, NEAR)
        sides, diag = own_part(place, own, mine, theirs)
        here, there = edge_part(place, [near], sides)
        return sides, diag, here, send(there, NEAR)

    sides, diag, near_tile, from_near = early(before_far, virt, own, *ring)
    here, back = edge_part(place, [most, last], sides)
    mine, there = last_part(place, [here, back, diag, near_tile, from_near], rest, sides)
    beside_of = lambda pairs: [(s, t ^ 4) for s, t in pairs]
    from_far = send(there, FAR) + send(there, beside_of(FAR))
    total = jnp.concatenate([mine + send(mine, beside_of(HERE)), from_far[None]])
    total = total + sum(lax.ppermute(total, "aux", [(a, a ^ k) for a in range(8)]) for k in (1, 2, 3))
    far_tile, diag, near_tile = flipped(total[0]) + total[4], total[1], flipped(total[2]) + total[3]
    far_tile, diag, near_tile = [t.reshape(20, 2, 20) for t in (far_tile, diag, near_tile)]
    before = jnp.where(core == 0, far_tile, near_tile)
    after = jnp.where(core == 0, near_tile, far_tile)
    return jnp.stack([before, diag, after], 2).transpose(1, 0, 2, 3)


def early(part, virt, *operands):
    def nothing(*operands):
        shapes = jax.eval_shape(part, *operands)
        return jax.tree.map(lambda s: jnp.zeros(s.shape, s.dtype), shapes)

    return lax.cond(virt < lax.axis_size("virt"), part, nothing, *operands)


def solution(mesh):
    placed = (P("aux", "virt", None), P(None, "aux", None))
    return jax.shard_map(
        body, mesh=mesh, in_specs=placed, out_specs=P(None, "virt", None, None), check_vma=False
    )
```

time: 402 us -> 104 us (0.26)
  waiting for transfers between devices: 303 us -> 19.6 us
  matrix products: 49.5 us -> 0 us
  Pallas kernels: 0 us -> 48.9 us
  blocking collectives: 32.6 us -> 0 us
  starting transfers between devices: 3.25 us -> 24.1 us
  between operations: 13.4 us -> 0.13 us
  local copies, waits for them, and re-layouts: 0.74 us -> 10.1 us
    ppermute x2 -> x19, waiting for transfers between devices: 254 us -> 19.6 us  [the longest x16 14.9 us: send(): return lax.ppermute(array, AXES, pairs)]
    dot_general x4 -> x0, matrix products: 49.5 us -> none  [the longest x3 34.5 us: make_tile(): jnp.einsum('pac,npbc->nab', factors, contracted, preferred_element_type=j...]
    pallas_call x0 -> x4, Pallas kernels: none -> 48.9 us  [the longest x1 25.3 us: own_part(): pl.pallas_call(own_kernel, in_specs=[pl.BlockSpec(memory_space=pltpu.SMEM...]
    all_gather x1 -> x0, waiting for transfers between devices: 47.8 us -> none  [body(): lambda_full = lax.all_gather(lambda_pairs, 'aux', axis=1, tiled=True)]
    psum x1 -> x0, blocking collectives: 32.6 us -> none  [body(): return lax.psum(stacked, 'aux')]
    ppermute x2 -> x19, starting transfers between devices: 3.25 us -> 24.1 us  [the longest x16 19.9 us: send(): return lax.ppermute(array, AXES, pairs)]
    dynamic_slice x0 -> x3, local copies, waits for them, and re-layouts: none -> 5.15 us  [the longest x2 5.14 us: part(): lax.dynamic_slice_in_dim(own, ((1 - core) * 7 + first) * ROWS, blocks * R...]
  transfers between devices with their start and end apart: 3 -> 19, of which waited for: 2 -> 12; matrix products, arithmetic and copies ran while one was open for 6% -> 7% of each run, Pallas kernels for 0% -> 45%
where the time goes in v2:
time: 104 us; the launch traced here: 103 us
  Pallas kernels  48.9 us (47%)
  starting transfers between devices  24.1 us (23%)
  waiting for transfers between devices  19.6 us (19%)
  local copies, waits for them, and re-layouts  10.1 us (10%)
    pallas_call x1, Pallas kernels, own_part(): pl.pallas_call(own_kernel, in_specs=[pl.BlockSpec(memory_space=pltpu.SMEM...  25.3 us
    pallas_call x2, Pallas kernels, edge_part(): pl.pallas_call(edge_kernel, grid_spec=pltpu.PrefetchScalarGridSpec(num_sc...  21.3 us
    ppermute x16, starting transfers between devices, send(): return lax.ppermute(array, AXES, pairs)  19.9 us
    ppermute x16, waiting for transfers between devices, send(): return lax.ppermute(array, AXES, pairs)  14.9 us
    dynamic_slice x2, local copies, waits for them, and re-layouts, part(): lax.dynamic_slice_in_dim(own, ((1 - core) * 7 + first) * ROWS, blocks * R...  5.14 us
    ppermute x3, waiting for transfers between devices, body(): lax.ppermute(total, 'aux', [(a, a ^ k) for a in range(8)])  4.65 us
    ppermute x3, starting transfers between devices, body(): lax.ppermute(total, 'aux', [(a, a ^ k) for a in range(8)])  4.18 us
    pallas_call x1, Pallas kernels, last_part(): pl.pallas_call(last_kernel, grid=(1,), in_specs=[pl.BlockSpec(memory_spac...  2.34 us
  transfers between devices with their start and end apart: 19, of which 12 were waited for; matrix products, arithmetic and copies ran while one was open for 7% of the time, Pallas kernels for 45%

profile of v2, /device:TPU:4, one launch (start us, length us, event | category | flops | bytes accessed | tf_op | source)
XLA Modules:
  0.0 102.9 jit_solution(10489457093675361481)
XLA Ops:
  0.9 1.3 %collective-permute-start.6 = (bf16[80,640]{1,0:T(8,128)(2,1)S(1)}, bf16[80,640]{1,0:T(8,128)(2,1)S(1)}, u32[]{:S(2)}, u32[]{:S(2)}) collective-permute-start(bf16[80,640]{1,0:T(8,128)(2,1)S(1)} %fusion.1), channel_id=1, source_target_pairs={{0,4},{1,5},{2,6},{3,7},{4,0},{5,1},{6,2},{7,3},{8,28},{9,29},{10,... | collective-permute-start | bytes 307208 | tf_op jit(solution)/shard_map/ppermute | solution.py:49
  2.2 3.3 %dynamic-slice_bitcast_fusion = bf16[20,96,640]{2,1,0:T(8,128)(2,1)} fusion(bf16[240,20,640]{2,0,1:T(8,128)(2,1)} %param.4, s32[]{:T(128)S(6)} %select_n.42), kind=kLoop, calls=%fused_computation | loop fusion | bytes 4915204 | tf_op jit(solution)/shard_map/dynamic_slice | solution.py:257
  5.7 1.1 %collective-permute-start.7 = (bf16[20,96,640]{2,1,0:T(8,128)(2,1)}, bf16[20,96,640]{2,1,0:T(8,128)(2,1)S(1)}, u32[]{:S(2)}, u32[]{:S(2)}) collective-permute-start(bf16[20,96,640]{2,1,0:T(8,128)(2,1)} %dynamic-slice_bitcast_fusion), channel_id=1, source_target_pairs={{0,248},{1,249},{2,250},{3,251},{4,252},{5,253},{6,254},{7,255},{8... | collective-permute-start | bytes 7372808 | tf_op jit(solution)/shard_map/ppermute | solution.py:49
  6.8 1.7 %collective-permute-start.10 = (bf16[2,80,640]{2,1,0:T(8,128)(2,1)S(1)}, bf16[2,80,640]{2,1,0:T(8,128)(2,1)S(1)}, u32[]{:S(2)}, u32[]{:S(2)}) collective-permute-start(bf16[2,80,640]{2,1,0:T(8,128)(2,1)S(1)} %pad_maximum_fusion), channel_id=1, source_target_pairs={{0,1},{1,2},{2,3},{3,0},{4,5},{5,6},{6,7},{7,4},{8,9},{9,10},{10,1... | collective-permute-start | bytes 614408 | tf_op jit(solution)/shard_map/ppermute | solution.py:49
  8.5 2.9 %collective-permute-start.9 = (bf16[2,80,640]{2,1,0:T(8,128)(2,1)S(1)}, bf16[2,80,640]{2,1,0:T(8,128)(2,1)S(1)}, u32[]{:S(2)}, u32[]{:S(2)}) collective-permute-start(bf16[2,80,640]{2,1,0:T(8,128)(2,1)S(1)} %pad_maximum_fusion), channel_id=1, source_target_pairs={{0,2},{1,3},{2,0},{3,1},{4,6},{5,7},{6,4},{7,5},{8,10},{9,11},{10,... | collective-permute-start | bytes 614408 | tf_op jit(solution)/shard_map/ppermute | solution.py:49
  11.4 1.3 %collective-permute-start.8 = (bf16[2,80,640]{2,1,0:T(8,128)(2,1)S(1)}, bf16[2,80,640]{2,1,0:T(8,128)(2,1)}, u32[]{:S(2)}, u32[]{:S(2)}) collective-permute-start(bf16[2,80,640]{2,1,0:T(8,128)(2,1)S(1)} %pad_maximum_fusion), channel_id=1, source_target_pairs={{0,3},{1,0},{2,1},{3,2},{4,7},{5,4},{6,5},{7,6},{8,11},{9,8},{10,9... | collective-permute-start | bytes 614408 | tf_op jit(solution)/shard_map/ppermute | solution.py:49
  12.7 1.8 %slice.24 = bf16[20,16,640]{2,1,0:T(8,128)(2,1)} slice(bf16[20,240,640]{2,1,0:T(8,128)(2,1)} %bitcast.31), slice={[0:20], [224:240], [0:640]} | slice | bytes 819200 | tf_op jit(solution)/shard_map/slice | solution.py:264
  14.6 1.8 %dynamic-slice_bitcast_fusion.1 = bf16[20,16,640]{2,1,0:T(8,128)(2,1)} fusion(bf16[240,20,640]{2,0,1:T(8,128)(2,1)} %param.4, s32[]{:T(128)S(6)} %select_n.43), kind=kLoop, calls=%fused_computation.1 | loop fusion | bytes 819204 | tf_op jit(solution)/shard_map/dynamic_slice | solution.py:257
  16.4 5.3 %collective-permute-done.9 = bf16[2,80,640]{2,1,0:T(8,128)(2,1)S(1)} collective-permute-done((bf16[2,80,640]{2,1,0:T(8,128)(2,1)S(1)}, bf16[2,80,640]{2,1,0:T(8,128)(2,1)S(1)}, u32[]{:S(2)}, u32[]{:S(2)}) %collective-permute-start.9) | collective-permute-done | bytes 204832 | tf_op jit(solution)/shard_map/ppermute | solution.py:49
  22.3 1.3 %collective-permute-start.11 = (bf16[20,16,640]{2,1,0:T(8,128)(2,1)}, bf16[20,16,640]{2,1,0:T(8,128)(2,1)S(1)}, u32[]{:S(2)}, u32[]{:S(2)}) collective-permute-start(bf16[20,16,640]{2,1,0:T(8,128)(2,1)} %slice.24), channel_id=1, source_target_pairs={{0,248},{1,249},{2,250},{3,251},{4,252},{5,253},{6,254},{7,255},{1... | collective-permute-start | bytes 1228808 | tf_op jit(solution)/shard_map/ppermute | solution.py:49
  23.9 45.8 %conditional.1 = (bf16[4,1280,1280]{2,1,0:T(8,128)(2,1)}, f32[20,40]{1,0:T(8,128)S(1)}, f32[20,40]{1,0:T(8,128)S(1)}, f32[20,40]{1,0:T(8,128)}) conditional(s32[]{:T(128)} %convert_element_type.3, () %tuple.19, (bf16[2,80,640]{2,1,0:T(8,128)(2,1)}, bf16[2,80,640]{2,1,0:T(8,128)(2,1)}, bf16[2,80,640]{2,1,0:T(8,128)(2,1)}, ...), branch_computations={%region_0.1_spmd, %region_1.2_spmd} | conditional | flops 2 | bytes 27865872 | solution.py:295
  23.9 4.9 %collective-permute-start = (bf16[2,80,640]{2,1,0:T(8,128)(2,1)}, bf16[2,80,640]{2,1,0:T(8,128)(2,1)S(1)}, u32[]{:S(2)}, u32[]{:S(2)}) collective-permute-start(bf16[2,80,640]{2,1,0:T(8,128)(2,1)} %get-tuple-element.19.refs_0_), channel_id=1, source_target_pairs={{0,8},{1,9},{2,10},{3,11},{4,12},{5,13},{6,14},{7,15},{8,0},{9,1},... | collective-permute-start | bytes 614408 | tf_op jit(solution)/shard_map/cond/branch_1_fun/ppermute | solution.py:49
  28.8 1.2 %collective-permute-done.refs_4_ = bf16[2,80,640]{2,1,0:T(8,128)(2,1)S(1)} collective-permute-done((bf16[2,80,640]{2,1,0:T(8,128)(2,1)}, bf16[2,80,640]{2,1,0:T(8,128)(2,1)S(1)}, u32[]{:S(2)}, u32[]{:S(2)}) %collective-permute-start) | collective-permute-done | bytes 204832 | tf_op jit(solution)/shard_map/cond/branch_1_fun/ppermute | solution.py:49
  30.9 1.2 %collective-permute-done.2.refs_6_ = bf16[2,80,640]{2,1,0:T(8,128)(2,1)S(1)} collective-permute-done((bf16[2,80,640]{2,1,0:T(8,128)(2,1)}, bf16[2,80,640]{2,1,0:T(8,128)(2,1)S(1)}, u32[]{:S(2)}, u32[]{:S(2)}) %collective-permute-start.2) | collective-permute-done | bytes 204832 | tf_op jit(solution)/shard_map/cond/branch_1_fun/ppermute | solution.py:49
  32.6 25.3 %own_part.1 = (bf16[4,1280,1280]{2,1,0:T(8,128)(2,1)}, f32[20,40]{1,0:T(8,128)S(1)}) custom-call(s32[3]{0:T(128)S(1)} %get-tuple-element.17.place_ref, bf16[20,240,640]{2,1,0:T(8,128)(2,1)} %get-tuple-element.33.f_hbm, bf16[2,80,640]{2,1,0:T(8,128)(2,1)} %get-tuple-element.19.refs_0_, bf16[2,80,640]{2,1,0:T(8,128)(2,1)} %get-tuple-element.20.refs_1_, ...), custom_call_target="tpu_custom_call" | custom-call | flops 1 | bytes 1 | tf_op jit(solution)/shard_map/cond/branch_1_fun/own_part/pallas_call | solution.py:145
  57.9 10.1 %edge_part.2 = (f32[20,40]{1,0:T(8,128)S(1)}, f32[20,40]{1,0:T(8,128)S(1)}) custom-call(s32[3]{0:T(128)S(1)} %get-tuple-element.17.place_ref, bf16[20,240,640]{2,1,0:T(8,128)(2,1)S(1)} %collective-permute-done.4.refs_0_.refs_1_, bf16[20,240,640]{2,1,0:T(8,128)(2,1)S(1)} %collective-permute-done.4.refs_0_.refs_1_, ...), custom_call_target="tpu_custom_call" | custom-call | flops 1 | bytes 1 | tf_op jit(solution)/shard_map/cond/branch_1_fun/edge_part/pallas_call | solution.py:202
  69.7 2.0 %collective-permute-done.7.refs_0_.refs_1_ = bf16[20,96,640]{2,1,0:T(8,128)(2,1)S(1)} collective-permute-done((bf16[20,96,640]{2,1,0:T(8,128)(2,1)}, bf16[20,96,640]{2,1,0:T(8,128)(2,1)S(1)}, u32[]{:S(2)}, u32[]{:S(2)}) %collective-permute-start.7) | collective-permute-done | bytes 2457632 | tf_op jit(solution)/shard_map/ppermute | solution.py:49
  71.7 11.2 %edge_part.3 = (f32[20,40]{1,0:T(8,128)S(1)}, f32[20,40]{1,0:T(8,128)S(1)}) custom-call(s32[3]{0:T(128)S(1)} %pad_add_fusion.place_ref, bf16[20,96,640]{2,1,0:T(8,128)(2,1)S(1)} %collective-permute-done.7.refs_0_.refs_1_, bf16[20,96,640]{2,1,0:T(8,128)(2,1)S(1)} %collective-permute-done.7.refs_0_.refs_1_, ...), custom_call_target="tpu_custom_call" | custom-call | flops 1 | bytes 1 | tf_op jit(solution)/shard_map/edge_part/pallas_call | solution.py:202
  82.9 2.3 %last_part.1 = (f32[4,20,40]{2,1,0:T(8,128)S(1)}, f32[20,40]{1,0:T(8,128)S(1)}) custom-call(s32[3]{0:T(128)S(1)} %pad_add_fusion.place_ref, f32[20,40]{1,0:T(8,128)S(1)} %get-tuple-element.60.here_ref, f32[20,40]{1,0:T(8,128)S(1)} %get-tuple-element.61.back_ref, f32[20,40]{1,0:T(8,128)S(1)} %get-tuple-element.62.diag_ref, ...), custom_call_target="tpu_custom_call" | custom-call | flops 1 | bytes 1 | tf_op jit(solution)/shard_map/last_part/pallas_call | solution.py:231
  85.3 3.1 %collective-permute-start.14 = (f32[20,40]{1,0:T(8,128)S(1)}, f32[20,40]{1,0:T(8,128)S(1)}, u32[]{:S(2)}, u32[]{:S(2)}) collective-permute-start(f32[20,40]{1,0:T(8,128)S(1)} %get-tuple-element.67), channel_id=1, source_target_pairs={{0,248},{1,249},{2,250},{3,251},{4,252},{5,253},{6,254},{7,255},{8... | collective-permute-start | bytes 9608 | tf_op jit(solution)/shard_map/ppermute | solution.py:49
  90.0 2.5 %collective-permute-done.13 = f32[4,20,40]{2,1,0:T(8,128)S(1)} collective-permute-done((f32[4,20,40]{2,1,0:T(8,128)S(1)}, f32[4,20,40]{2,1,0:T(8,128)S(1)}, u32[]{:S(2)}, u32[]{:S(2)}) %collective-permute-start.13) | collective-permute-done | bytes 12832 | tf_op jit(solution)/shard_map/ppermute | solution.py:49
  92.5 3.1 %collective-permute-start.18 = (f32[5,20,40]{2,1,0:T(8,128)S(1)}, f32[5,20,40]{2,1,0:T(8,128)S(1)}, u32[]{:S(2)}, u32[]{:S(2)}) collective-permute-start(f32[5,20,40]{2,1,0:T(8,128)S(1)} %pad_maximum_fusion.1), channel_id=1, source_target_pairs={{0,3},{1,2},{2,1},{3,0},{4,7},{5,6},{6,5},{7,4},{8,11},{9,10},{10,... | collective-permute-start | bytes 48008 | tf_op jit(solution)/shard_map/ppermute | solution.py:282
  96.7 1.3 %collective-permute-done.18 = f32[5,20,40]{2,1,0:T(8,128)S(1)} collective-permute-done((f32[5,20,40]{2,1,0:T(8,128)S(1)}, f32[5,20,40]{2,1,0:T(8,128)S(1)}, u32[]{:S(2)}, u32[]{:S(2)}) %collective-permute-start.18) | collective-permute-done | bytes 16032 | tf_op jit(solution)/shard_map/ppermute | solution.py:282
  98.0 3.3 %collective-permute-done.17 = f32[5,20,40]{2,1,0:T(8,128)S(1)} collective-permute-done((f32[5,20,40]{2,1,0:T(8,128)S(1)}, f32[5,20,40]{2,1,0:T(8,128)S(1)}, u32[]{:S(2)}, u32[]{:S(2)}) %collective-permute-start.17) | collective-permute-done | bytes 16032 | tf_op jit(solution)/shard_map/ppermute | solution.py:282
  (52 shorter events, 9.5 us)
Async XLA Ops:
  0.0 0.9 copy-start
  0.9 4.7 %collective-permute-start.6 = (bf16[80,640]{1,0:T(8,128)(2,1)S(1)}, bf16[80,640]{1,0:T(8,128)(2,1)S(1)}, u32[]{:S(2)}, u32[]{:S(2)}) collective-permute-start(bf16[80,640]{1,0:T(8,128)(2,1)S(1)} %fusion.1), channel_id=1, source_target_pairs={{0,4},{1,5},{2,6},{3,7},{4,0},{5,1},{6,2},{7,3},{8,28},{9,29},{10,... | collective-permute-start | bytes 307208 | tf_op jit(solution)/shard_map/ppermute | solution.py:49
  5.7 66.0 %collective-permute-start.7 = (bf16[20,96,640]{2,1,0:T(8,128)(2,1)}, bf16[20,96,640]{2,1,0:T(8,128)(2,1)S(1)}, u32[]{:S(2)}, u32[]{:S(2)}) collective-permute-start(bf16[20,96,640]{2,1,0:T(8,128)(2,1)} %dynamic-slice_bitcast_fusion), channel_id=1, source_target_pairs={{0,248},{1,249},{2,250},{3,251},{4,252},{5,253},{6,254},{7,255},{8... | collective-permute-start | bytes 7372808 | tf_op jit(solution)/shard_map/ppermute | solution.py:49
  6.8 15.5 %copy-start.2 = (bf16[2,80,640]{2,1,0:T(8,128)(2,1)}, bf16[2,80,640]{2,1,0:T(8,128)(2,1)S(1)}, u32[]{:S(2)}) copy-start(bf16[2,80,640]{2,1,0:T(8,128)(2,1)S(1)} %pad_maximum_fusion) | copy-start | bytes 614404
  6.8 9.5 %collective-permute-start.10 = (bf16[2,80,640]{2,1,0:T(8,128)(2,1)S(1)}, bf16[2,80,640]{2,1,0:T(8,128)(2,1)S(1)}, u32[]{:S(2)}, u32[]{:S(2)}) collective-permute-start(bf16[2,80,640]{2,1,0:T(8,128)(2,1)S(1)} %pad_maximum_fusion), channel_id=1, source_target_pairs={{0,1},{1,2},{2,3},{3,0},{4,5},{5,6},{6,7},{7,4},{8,9},{9,10},{10,1... | collective-permute-start | bytes 614408 | tf_op jit(solution)/shard_map/ppermute | solution.py:49
  8.5 13.1 %collective-permute-start.9 = (bf16[2,80,640]{2,1,0:T(8,128)(2,1)S(1)}, bf16[2,80,640]{2,1,0:T(8,128)(2,1)S(1)}, u32[]{:S(2)}, u32[]{:S(2)}) collective-permute-start(bf16[2,80,640]{2,1,0:T(8,128)(2,1)S(1)} %pad_maximum_fusion), channel_id=1, source_target_pairs={{0,2},{1,3},{2,0},{3,1},{4,6},{5,7},{6,4},{7,5},{8,10},{9,11},{10,... | collective-permute-start | bytes 614408 | tf_op jit(solution)/shard_map/ppermute | solution.py:49
  11.4 10.9 %collective-permute-start.8 = (bf16[2,80,640]{2,1,0:T(8,128)(2,1)S(1)}, bf16[2,80,640]{2,1,0:T(8,128)(2,1)}, u32[]{:S(2)}, u32[]{:S(2)}) collective-permute-start(bf16[2,80,640]{2,1,0:T(8,128)(2,1)S(1)} %pad_maximum_fusion), channel_id=1, source_target_pairs={{0,3},{1,0},{2,1},{3,2},{4,7},{5,4},{6,5},{7,6},{8,11},{9,8},{10,9... | collective-permute-start | bytes 614408 | tf_op jit(solution)/shard_map/ppermute | solution.py:49
  16.4 6.0 %copy-start.3 = (bf16[2,80,640]{2,1,0:T(8,128)(2,1)}, bf16[2,80,640]{2,1,0:T(8,128)(2,1)S(1)}, u32[]{:S(2)}) copy-start(bf16[2,80,640]{2,1,0:T(8,128)(2,1)S(1)} %collective-permute-done.10) | copy-start | bytes 614404
  21.6 0.7 copy-start.4
  22.3 47.3 %collective-permute-start.11 = (bf16[20,16,640]{2,1,0:T(8,128)(2,1)}, bf16[20,16,640]{2,1,0:T(8,128)(2,1)S(1)}, u32[]{:S(2)}, u32[]{:S(2)}) collective-permute-start(bf16[20,16,640]{2,1,0:T(8,128)(2,1)} %slice.24), channel_id=1, source_target_pairs={{0,248},{1,249},{2,250},{3,251},{4,252},{5,253},{6,254},{7,255},{1... | collective-permute-start | bytes 1228808 | tf_op jit(solution)/shard_map/ppermute | solution.py:49
  23.7 59.2 %collective-permute-start.12 = (bf16[20,16,640]{2,1,0:T(8,128)(2,1)}, bf16[20,16,640]{2,1,0:T(8,128)(2,1)S(1)}, u32[]{:S(2)}, u32[]{:S(2)}) collective-permute-start(bf16[20,16,640]{2,1,0:T(8,128)(2,1)} %dynamic-slice_bitcast_fusion.1), channel_id=1, source_target_pairs={{0,248},{1,249},{2,250},{3,251},{4,252},{5,253},{6,254},{7,255},{8... | collective-permute-start | bytes 1228808 | tf_op jit(solution)/shard_map/ppermute | solution.py:49
  23.9 6.2 %collective-permute-start = (bf16[2,80,640]{2,1,0:T(8,128)(2,1)}, bf16[2,80,640]{2,1,0:T(8,128)(2,1)S(1)}, u32[]{:S(2)}, u32[]{:S(2)}) collective-permute-start(bf16[2,80,640]{2,1,0:T(8,128)(2,1)} %get-tuple-element.19.refs_0_), channel_id=1, source_target_pairs={{0,8},{1,9},{2,10},{3,11},{4,12},{5,13},{6,14},{7,15},{8,0},{9,1},... | collective-permute-start | bytes 614408 | tf_op jit(solution)/shard_map/cond/branch_1_fun/ppermute | solution.py:49
  28.7 1.7 %collective-permute-start.1 = (bf16[2,80,640]{2,1,0:T(8,128)(2,1)}, bf16[2,80,640]{2,1,0:T(8,128)(2,1)S(1)}, u32[]{:S(2)}, u32[]{:S(2)}) collective-permute-start(bf16[2,80,640]{2,1,0:T(8,128)(2,1)} %get-tuple-element.20.refs_1_), channel_id=1, source_target_pairs={{0,8},{1,9},{2,10},{3,11},{4,12},{5,13},{6,14},{7,15},{8,0},{9,1},... | collective-permute-start | bytes 614408 | tf_op jit(solution)/shard_map/cond/branch_1_fun/ppermute | solution.py:49
  30.4 1.7 %collective-permute-start.2 = (bf16[2,80,640]{2,1,0:T(8,128)(2,1)}, bf16[2,80,640]{2,1,0:T(8,128)(2,1)S(1)}, u32[]{:S(2)}, u32[]{:S(2)}) collective-permute-start(bf16[2,80,640]{2,1,0:T(8,128)(2,1)} %get-tuple-element.25.refs_2_), channel_id=1, source_target_pairs={{0,8},{1,9},{2,10},{3,11},{4,12},{5,13},{6,14},{7,15},{8,0},{9,1},... | collective-permute-start | bytes 614408 | tf_op jit(solution)/shard_map/cond/branch_1_fun/ppermute | solution.py:49
  30.7 1.7 %collective-permute-start.3 = (bf16[2,80,640]{2,1,0:T(8,128)(2,1)}, bf16[2,80,640]{2,1,0:T(8,128)(2,1)S(1)}, u32[]{:S(2)}, u32[]{:S(2)}) collective-permute-start(bf16[2,80,640]{2,1,0:T(8,128)(2,1)} %get-tuple-element.26.refs_3_), channel_id=1, source_target_pairs={{0,8},{1,9},{2,10},{3,11},{4,12},{5,13},{6,14},{7,15},{8,0},{9,1},... | collective-permute-start | bytes 614408 | tf_op jit(solution)/shard_map/cond/branch_1_fun/ppermute | solution.py:49
  32.4 25.6 %collective-permute-start.4 = (bf16[20,240,640]{2,1,0:T(8,128)(2,1)}, bf16[20,240,640]{2,1,0:T(8,128)(2,1)S(1)}, u32[]{:S(2)}, u32[]{:S(2)}) collective-permute-start(bf16[20,240,640]{2,1,0:T(8,128)(2,1)} %get-tuple-element.33.f_hbm), channel_id=1, source_target_pairs={{0,8},{1,9},{2,10},{3,11},{4,12},{5,13},{6,14},{7,15},{8,0},{9,1},... | collective-permute-start | bytes 18432008 | tf_op jit(solution)/shard_map/cond/branch_1_fun/ppermute | solution.py:49
  68.0 1.6 %collective-permute-start.5 = (f32[20,40]{1,0:T(8,128)S(1)}, f32[20,40]{1,0:T(8,128)}, u32[]{:S(2)}, u32[]{:S(2)}) collective-permute-start(f32[20,40]{1,0:T(8,128)S(1)} %get-tuple-element.35), channel_id=1, source_target_pairs={{0,8},{1,9},{2,10},{3,11},{4,12},{5,13},{6,14},{7,15},{8,0},{9,1},... | collective-permute-start | bytes 9608 | tf_op jit(solution)/shard_map/cond/branch_1_fun/ppermute | solution.py:49
  71.7 11.2 %copy-start.1 = (bf16[4,1280,1280]{2,1,0:T(8,128)(2,1)S(1)}, bf16[4,1280,1280]{2,1,0:T(8,128)(2,1)}, u32[]{:S(2)}) copy-start(bf16[4,1280,1280]{2,1,0:T(8,128)(2,1)} %get-tuple-element.59.refs_3_.side_ref) | copy-start | bytes 39321604
  85.2 3.9 %collective-permute-start.15 = (f32[20,40]{1,0:T(8,128)S(1)}, f32[20,40]{1,0:T(8,128)S(1)}, u32[]{:S(2)}, u32[]{:S(2)}) collective-permute-start(f32[20,40]{1,0:T(8,128)S(1)} %get-tuple-element.67), channel_id=1, source_target_pairs={{0,252},{1,253},{2,254},{3,255},{4,248},{5,249},{6,250},{7,251},{8... | collective-permute-start | bytes 9608 | tf_op jit(solution)/shard_map/ppermute | solution.py:49
  85.3 4.7 %collective-permute-start.14 = (f32[20,40]{1,0:T(8,128)S(1)}, f32[20,40]{1,0:T(8,128)S(1)}, u32[]{:S(2)}, u32[]{:S(2)}) collective-permute-start(f32[20,40]{1,0:T(8,128)S(1)} %get-tuple-element.67), channel_id=1, source_target_pairs={{0,248},{1,249},{2,250},{3,251},{4,252},{5,253},{6,254},{7,255},{8... | collective-permute-start | bytes 9608 | tf_op jit(solution)/shard_map/ppermute | solution.py:49
  88.4 4.1 %collective-permute-start.13 = (f32[4,20,40]{2,1,0:T(8,128)S(1)}, f32[4,20,40]{2,1,0:T(8,128)S(1)}, u32[]{:S(2)}, u32[]{:S(2)}) collective-permute-start(f32[4,20,40]{2,1,0:T(8,128)S(1)} %get-tuple-element.66), channel_id=1, source_target_pairs={{0,4},{1,5},{2,6},{3,7},{4,0},{5,1},{6,2},{7,3},{8,12},{9,13},{10,... | collective-permute-start | bytes 38408 | tf_op jit(solution)/shard_map/ppermute | solution.py:49
  92.5 5.5 %collective-permute-start.18 = (f32[5,20,40]{2,1,0:T(8,128)S(1)}, f32[5,20,40]{2,1,0:T(8,128)S(1)}, u32[]{:S(2)}, u32[]{:S(2)}) collective-permute-start(f32[5,20,40]{2,1,0:T(8,128)S(1)} %pad_maximum_fusion.1), channel_id=1, source_target_pairs={{0,3},{1,2},{2,1},{3,0},{4,7},{5,6},{6,5},{7,4},{8,11},{9,10},{10,... | collective-permute-start | bytes 48008 | tf_op jit(solution)/shard_map/ppermute | solution.py:282
  95.6 5.7 %collective-permute-start.17 = (f32[5,20,40]{2,1,0:T(8,128)S(1)}, f32[5,20,40]{2,1,0:T(8,128)S(1)}, u32[]{:S(2)}, u32[]{:S(2)}) collective-permute-start(f32[5,20,40]{2,1,0:T(8,128)S(1)} %pad_maximum_fusion.1), channel_id=1, source_target_pairs={{0,2},{1,3},{2,0},{3,1},{4,6},{5,7},{6,4},{7,5},{8,10},{9,11},{10,... | collective-permute-start | bytes 48008 | tf_op jit(solution)/shard_map/ppermute | solution.py:282
  96.4 5.0 %collective-permute-start.16 = (f32[5,20,40]{2,1,0:T(8,128)S(1)}, f32[5,20,40]{2,1,0:T(8,128)S(1)}, u32[]{:S(2)}, u32[]{:S(2)}) collective-permute-start(f32[5,20,40]{2,1,0:T(8,128)S(1)} %pad_maximum_fusion.1), channel_id=1, source_target_pairs={{0,1},{1,0},{2,3},{3,2},{4,5},{5,4},{6,7},{7,6},{8,9},{9,8},{10,11... | collective-permute-start | bytes 48008 | tf_op jit(solution)/shard_map/ppermute | solution.py:282
